TPU v7x, 32 devices: a whole 2x2x4 slice. The times are simulated.
32 devices in a mesh: fsdp: 8 (over z, y), rep: 4 (over x, core).
Axes of the slice: x: 2, y: 2, z: 4, core: 2. Of those that a mesh axis runs over, the one named last changes fastest.
Arguments:
- latents: bfloat16 [3, 64, 256, 384], P(None, ('fsdp', 'rep')), may hold values from -6 to 6
- cotangent: bfloat16 [3, 64, 256, 384], P(None, ('fsdp', 'rep')), may hold values from -6 to 6
- counts: int32 [3, 32], P(None, ('fsdp', 'rep')), may hold values from 1 to 2, 48 in all within a row
- labels: int32 [3, 64], P(None, ('fsdp', 'rep')), may hold values from 0 to 999
- timesteps: int32 [3, 64], P(None, ('fsdp', 'rep')), may hold values from 0 to 999
- class_table: bfloat16 [1000, 384], P(None, 'fsdp'), may hold values from -5 to 5
- time_table: bfloat16 [1000, 384], P(None, 'fsdp'), may hold values from -5 to 5
- ada_weight: bfloat16 [2, 384, 2304], P(None, 'fsdp'), may hold values from -0.3125 to 0.3125
- ada_bias: bfloat16 [2, 2304], P(None, 'fsdp'), may hold values from -3 to 3
- qkv_weight: bfloat16 [2, 384, 1152], P(None, 'fsdp'), may hold values from -0.3125 to 0.3125
- qv_bias: bfloat16 [2, 768], P(None, 'fsdp'), may hold values from -3 to 3
- proj_weight: bfloat16 [2, 384, 384], P(None, 'fsdp'), may hold values from -1.25 to 1.25
- proj_bias: bfloat16 [2, 384], P(None, 'fsdp'), may hold values from -3 to 3
- fc1_weight: bfloat16 [2, 384, 1536], P(None, 'fsdp'), may hold values from -0.3125 to 0.3125
- fc1_bias: bfloat16 [2, 1536], P(None, 'fsdp'), may hold values from -3 to 3
- fc2_weight: bfloat16 [2, 1536, 384], P(None, 'fsdp'), may hold values from -0.15625 to 0.15625
- fc2_bias: bfloat16 [2, 384], P(None, 'fsdp'), may hold values from -3 to 3
Outputs:
- outputs: bfloat16 [3, 64, 256, 384], P(None, ('fsdp', 'rep'))
- input_grad: bfloat16 [3, 64, 256, 384], P(None, ('fsdp', 'rep'))
- class_grad: float32 [1000, 384], P(None, 'fsdp')
- time_grad: float32 [1000, 384], P(None, 'fsdp')
- ada_weight_grad: float32 [2, 384, 2304], P(None, 'fsdp')
- ada_bias_grad: float32 [2, 2304], P(None, 'fsdp')
- qkv_weight_grad: float32 [2, 384, 1152], P(None, 'fsdp')
- qv_bias_grad: float32 [2, 768], P(None, 'fsdp')
- proj_weight_grad: float32 [2, 384, 384], P(None, 'fsdp')
- proj_bias_grad: float32 [2, 384], P(None, 'fsdp')
- fc1_weight_grad: float32 [2, 384, 1536], P(None, 'fsdp')
- fc1_bias_grad: float32 [2, 1536], P(None, 'fsdp')
- fc2_weight_grad: float32 [2, 1536, 384], P(None, 'fsdp')
- fc2_bias_grad: float32 [2, 384], P(None, 'fsdp')
Inputs may be any that keep to these rules, and one draw needn't show every extreme that they name: A device's live latents are its first slots; the counts of one micro-batch add up to 48, and some device holds 2.
All inputs are finite; a program needn't handle non-finite values.
Results may differ from a plain program's by a relative error of at most 0.017.
Values may be sent and summed in bfloat16 or wider, within the bound.
A program may use at most 192 MiB of HBM per device.

v0:
```python
from functools import partial

import jax
import jax.numpy as jnp
from jax import lax
from jax.sharding import PartitionSpec as P

HEADS = 6
LAYERS = 2


highest = lax.Precision.HIGHEST
epsilon = 1e-06


def layer_norm(values):
    centre = jnp.mean(values, axis=-1, keepdims=True)
    centred = values - centre
    spread = jnp.mean(centred * centred, axis=-1, keepdims=True)
    return centred * lax.rsqrt(spread + epsilon)


def split_weights(gathered, layer_index):
    return tuple((member[layer_index] for member in gathered[2:]))


def attend(queries, key_rows, value_rows):
    length, features = queries.shape
    head_size = features // HEADS
    score_scale = head_size ** (-0.5)
    query_h = queries.reshape(length, HEADS, head_size)
    key_h = key_rows.reshape(length, HEADS, head_size)
    value_h = value_rows.reshape(length, HEADS, head_size)
    scores = (
        jnp.einsum("qhe,khe->hqk", query_h, key_h, preferred_element_type=jnp.float32) * score_scale
    )
    top_score = jnp.max(scores, axis=-1, keepdims=True)
    raised = jnp.exp(scores - top_score)
    soft = raised / jnp.sum(raised, axis=-1, keepdims=True)
    soft_r = soft.astype(jnp.bfloat16)
    blended = jnp.einsum("hqk,khe->qhe", soft_r, value_h, preferred_element_type=jnp.float32)
    return (soft, soft_r, blended.reshape(length, features))


def layer_parts(residual, lift_row, layer_w):
    ada_w, ada_b, qkv_w, qv_b, proj_w, proj_b, fc1_w, fc1_b, fc2_w, fc2_b = layer_w
    features = residual.shape[-1]
    modulation = jnp.dot(lift_row[None, :], ada_w, preferred_element_type=jnp.float32)[
        0
    ] + ada_b.astype(jnp.float32)
    pieces = [modulation[column * features : (column + 1) * features] for column in range(6)]
    shift_a, scale_a, gate_a, shift_m, scale_m, gate_m = pieces
    normed_a = layer_norm(residual)
    moved_a = (normed_a * (1.0 + scale_a) + shift_a).astype(jnp.bfloat16)
    projected = jnp.dot(moved_a, qkv_w, preferred_element_type=jnp.float32)
    bias_qv = qv_b.astype(jnp.float32)
    queries = (projected[:, :features] + bias_qv[:features]).astype(jnp.bfloat16)
    key_rows = projected[:, features : 2 * features].astype(jnp.bfloat16)
    value_rows = (projected[:, 2 * features :] + bias_qv[features:]).astype(jnp.bfloat16)
    soft, soft_r, blended = attend(queries, key_rows, value_rows)
    blended_r = blended.astype(jnp.bfloat16)
    branch = jnp.dot(blended_r, proj_w, preferred_element_type=jnp.float32) + proj_b.astype(
        jnp.float32
    )
    middle = residual + gate_a * branch
    normed_m = layer_norm(middle)
    moved_m = (normed_m * (1.0 + scale_m) + shift_m).astype(jnp.bfloat16)
    hidden_input_rows = jnp.dot(moved_m, fc1_w, preferred_element_type=jnp.float32) + fc1_b.astype(
        jnp.float32
    )
    hidden = jax.nn.gelu(hidden_input_rows, approximate=True).astype(jnp.bfloat16)
    mlp_out = jnp.dot(hidden, fc2_w, preferred_element_type=jnp.float32) + fc2_b.astype(jnp.float32)
    output = middle + gate_m * mlp_out
    return {
        "scale_a": scale_a,
        "gate_a": gate_a,
        "scale_m": scale_m,
        "gate_m": gate_m,
        "normed_a": normed_a,
        "moved_a": moved_a,
        "queries": queries,
        "key_rows": key_rows,
        "value_rows": value_rows,
        "soft": soft,
        "soft_r": soft_r,
        "blended_r": blended_r,
        "branch": branch,
        "middle": middle,
        "normed_m": normed_m,
        "moved_m": moved_m,
        "hidden_in": hidden_input_rows,
        "hidden": hidden,
        "mlp_out": mlp_out,
        "output": output,
    }


def layer_back(residual, lift_row, layer_w, grad_out):
    parts = layer_parts(residual, lift_row, layer_w)
    ada_w, ada_b, qkv_w, qv_b, proj_w, proj_b, fc1_w, fc1_b, fc2_w, fc2_b = layer_w
    length, features = residual.shape
    head_size = features // HEADS
    score_scale = head_size ** (-0.5)
    grad_gate_m = jnp.sum(grad_out * parts["mlp_out"], axis=0)
    grad_mlp = (parts["gate_m"] * grad_out).astype(jnp.bfloat16)
    grad_fc2_w = jnp.dot(parts["hidden"].T, grad_mlp, preferred_element_type=jnp.float32)
    grad_fc2_b = jnp.sum(grad_mlp.astype(jnp.float32), axis=0)
    grad_hidden = jnp.dot(grad_mlp, fc2_w.T, preferred_element_type=jnp.float32)
    discarded_value, gelu_pull = jax.vjp(partial(jax.nn.gelu, approximate=True), parts["hidden_in"])
    grad_hidden_in = gelu_pull(grad_hidden)[0].astype(jnp.bfloat16)
    grad_fc1_w = jnp.dot(parts["moved_m"].T, grad_hidden_in, preferred_element_type=jnp.float32)
    grad_fc1_b = jnp.sum(grad_hidden_in.astype(jnp.float32), axis=0)
    grad_moved_m = jnp.dot(grad_hidden_in, fc1_w.T, preferred_element_type=jnp.float32)
    grad_shift_m = jnp.sum(grad_moved_m, axis=0)
    grad_scale_m = jnp.sum(grad_moved_m * parts["normed_m"], axis=0)
    discarded_value, norm_pull_m = jax.vjp(layer_norm, parts["middle"])
    grad_middle = grad_out + norm_pull_m(grad_moved_m * (1.0 + parts["scale_m"]))[0]
    grad_gate_a = jnp.sum(grad_middle * parts["branch"], axis=0)
    grad_branch = (parts["gate_a"] * grad_middle).astype(jnp.bfloat16)
    grad_proj_w = jnp.dot(parts["blended_r"].T, grad_branch, preferred_element_type=jnp.float32)
    grad_proj_b = jnp.sum(grad_branch.astype(jnp.float32), axis=0)
    mixed_output_gradient = jnp.dot(
        grad_branch, proj_w.T, preferred_element_type=jnp.float32
    ).astype(jnp.bfloat16)
    mixed_output_gradient = mixed_output_gradient.reshape(length, HEADS, head_size)
    query_h = parts["queries"].reshape(length, HEADS, head_size)
    key_h = parts["key_rows"].reshape(length, HEADS, head_size)
    value_h = parts["value_rows"].reshape(length, HEADS, head_size)
    soft = parts["soft"]
    grad_soft = jnp.einsum(
        "qhe,khe->hqk", mixed_output_gradient, value_h, preferred_element_type=jnp.float32
    )
    grad_value = jnp.einsum(
        "hqk,qhe->khe", parts["soft_r"], mixed_output_gradient, preferred_element_type=jnp.float32
    )
    grad_value = grad_value.reshape(length, features).astype(jnp.bfloat16)
    grad_scores = (soft * (grad_soft - jnp.sum(grad_soft * soft, axis=-1, keepdims=True))).astype(
        jnp.bfloat16
    )
    grad_query = (
        jnp.einsum("hqk,khe->qhe", grad_scores, key_h, preferred_element_type=jnp.float32)
        * score_scale
    )
    grad_query = grad_query.reshape(length, features).astype(jnp.bfloat16)
    grad_key = (
        jnp.einsum("hqk,qhe->khe", grad_scores, query_h, preferred_element_type=jnp.float32)
        * score_scale
    )
    grad_key = grad_key.reshape(length, features).astype(jnp.bfloat16)
    grad_projected = jnp.concatenate([grad_query, grad_key, grad_value], axis=1)
    grad_qkv_w = jnp.dot(parts["moved_a"].T, grad_projected, preferred_element_type=jnp.float32)
    grad_qv_b = jnp.concatenate(
        [
            jnp.sum(grad_query.astype(jnp.float32), axis=0),
            jnp.sum(grad_value.astype(jnp.float32), axis=0),
        ]
    )
    grad_moved_a = jnp.dot(grad_projected, qkv_w.T, preferred_element_type=jnp.float32)
    grad_shift_a = jnp.sum(grad_moved_a, axis=0)
    grad_scale_a = jnp.sum(grad_moved_a * parts["normed_a"], axis=0)
    discarded_value, norm_pull_a = jax.vjp(layer_norm, residual)
    grad_input = grad_middle + norm_pull_a(grad_moved_a * (1.0 + parts["scale_a"]))[0]
    grad_mod = jnp.concatenate(
        [grad_shift_a, grad_scale_a, grad_gate_a, grad_shift_m, grad_scale_m, grad_gate_m]
    )
    lift_full = lift_row.astype(jnp.float32)
    grad_ada_w = lift_full[:, None] * grad_mod[None, :]
    grad_lift = jnp.dot(ada_w.astype(jnp.float32), grad_mod, precision=highest)
    layer_grads = (
        grad_ada_w,
        grad_mod,
        grad_qkv_w,
        grad_qv_b,
        grad_proj_w,
        grad_proj_b,
        grad_fc1_w,
        grad_fc1_b,
        grad_fc2_w,
        grad_fc2_b,
    )
    return (grad_input, grad_lift, layer_grads)


def forward_slot(gathered, block_input_state, lift_row, alive_flag):

    def forward_run_slot(block):
        residual = block.astype(jnp.float32)
        saved = []
        for layer_index in range(LAYERS):
            saved.append(residual)
            residual = layer_parts(residual, lift_row, split_weights(gathered, layer_index))[
                "output"
            ]
        return (residual.astype(jnp.bfloat16), jnp.stack(saved))

    def forward_skip_slot(block):
        return (
            jnp.zeros(block.shape, jnp.bfloat16),
            jnp.zeros((LAYERS,) + block.shape, jnp.float32),
        )

    return lax.cond(alive_flag, forward_run_slot, forward_skip_slot, block_input_state)


def backward_slot(gathered, saved, lift_row, cond_row, grad_row, alive_flag, totals):

    def backward_run_slot(totals):
        grad_state = grad_row.astype(jnp.float32)
        lift_grad = jnp.zeros(cond_row.shape, jnp.float32)
        per_layer = [None] * LAYERS
        for layer_index in reversed(range(LAYERS)):
            grad_state, lift_part, per_layer[layer_index] = layer_back(
                saved[layer_index], lift_row, split_weights(gathered, layer_index), grad_state
            )
            lift_grad = lift_grad + lift_part
        stacked = tuple(
            (
                jnp.stack([per_layer[depth_at][member] for depth_at in range(LAYERS)])
                for member in range(10)
            )
        )
        updated = tuple((earlier + addition for earlier, addition in zip(totals, stacked)))
        discarded_value, silu_pull = jax.vjp(jax.nn.silu, cond_row)
        return (updated, (grad_state.astype(jnp.bfloat16), silu_pull(lift_grad)[0]))

    def backward_skip_slot(totals):
        return (
            totals,
            (jnp.zeros(grad_row.shape, jnp.bfloat16), jnp.zeros(cond_row.shape, jnp.float32)),
        )

    return lax.cond(alive_flag, backward_run_slot, backward_skip_slot, totals)


def on_device(
    latents,
    cotangent,
    counts,
    labels,
    timesteps,
    class_table,
    time_table,
    ada_weight,
    ada_bias,
    qkv_weight,
    qv_bias,
    proj_weight,
    proj_bias,
    fc1_weight,
    fc1_bias,
    fc2_weight,
    fc2_bias,
):
    micro_count, slot_count, length, features = latents.shape
    owners = lax.axis_size("fsdp")
    shard_list = (
        ada_weight,
        ada_bias,
        qkv_weight,
        qv_bias,
        proj_weight,
        proj_bias,
        fc1_weight,
        fc1_bias,
        fc2_weight,
        fc2_bias,
    )
    totals = tuple(
        (
            jnp.zeros((member.shape[0], member.shape[1] * owners) + member.shape[2:], jnp.float32)
            for member in shard_list
        )
    )
    out_list = []
    grad_list = []
    dcond_list = []
    slot_ids = jnp.arange(slot_count, dtype=jnp.int32)
    for micro_index in range(micro_count):
        forward_w = (
            lax.all_gather(class_table, "fsdp", axis=1, tiled=True),
            lax.all_gather(time_table, "fsdp", axis=1, tiled=True),
            lax.all_gather(ada_weight, "fsdp", axis=1, tiled=True),
            lax.all_gather(ada_bias, "fsdp", axis=1, tiled=True),
            lax.all_gather(qkv_weight, "fsdp", axis=1, tiled=True),
            lax.all_gather(qv_bias, "fsdp", axis=1, tiled=True),
            lax.all_gather(proj_weight, "fsdp", axis=1, tiled=True),
            lax.all_gather(proj_bias, "fsdp", axis=1, tiled=True),
            lax.all_gather(fc1_weight, "fsdp", axis=1, tiled=True),
            lax.all_gather(fc1_bias, "fsdp", axis=1, tiled=True),
            lax.all_gather(fc2_weight, "fsdp", axis=1, tiled=True),
            lax.all_gather(fc2_bias, "fsdp", axis=1, tiled=True),
        )
        condition_vector = jnp.take(forward_w[0], labels[micro_index], axis=0).astype(
            jnp.float32
        ) + jnp.take(forward_w[1], timesteps[micro_index], axis=0).astype(jnp.float32)
        lifted = jax.nn.silu(condition_vector).astype(jnp.bfloat16)
        alive = slot_ids < counts[micro_index, 0]

        def forward_step(carry, element, weights_now=forward_w):
            block_input_state, lift_row, alive_flag = element
            return (carry, forward_slot(weights_now, block_input_state, lift_row, alive_flag))

        discarded_value, (block_outs, saved) = lax.scan(
            forward_step, 0, (latents[micro_index], lifted, alive)
        )
        out_list.append(block_outs)
        backward_w = (
            lax.all_gather(class_table, "fsdp", axis=1, tiled=True),
            lax.all_gather(time_table, "fsdp", axis=1, tiled=True),
            lax.all_gather(ada_weight, "fsdp", axis=1, tiled=True),
            lax.all_gather(ada_bias, "fsdp", axis=1, tiled=True),
            lax.all_gather(qkv_weight, "fsdp", axis=1, tiled=True),
            lax.all_gather(qv_bias, "fsdp", axis=1, tiled=True),
            lax.all_gather(proj_weight, "fsdp", axis=1, tiled=True),
            lax.all_gather(proj_bias, "fsdp", axis=1, tiled=True),
            lax.all_gather(fc1_weight, "fsdp", axis=1, tiled=True),
            lax.all_gather(fc1_bias, "fsdp", axis=1, tiled=True),
            lax.all_gather(fc2_weight, "fsdp", axis=1, tiled=True),
            lax.all_gather(fc2_bias, "fsdp", axis=1, tiled=True),
        )

        def backward_step(carry, element, weights_now=backward_w):
            saved_in, lift_row, cond_row, grad_row, alive_flag = element
            return backward_slot(
                weights_now, saved_in, lift_row, cond_row, grad_row, alive_flag, carry
            )

        totals, (grad_blocks, dcond_rows) = lax.scan(
            backward_step, totals, (saved, lifted, condition_vector, cotangent[micro_index], alive)
        )
        grad_list.append(grad_blocks)
        dcond_list.append(dcond_rows)
    all_dcond = jnp.concatenate(dcond_list, axis=0)
    label_flat = labels.reshape(-1)
    step_flat = timesteps.reshape(-1)
    label_hot = (
        label_flat[:, None] == jnp.arange(class_table.shape[0], dtype=jnp.int32)[None, :]
    ).astype(jnp.float32)
    step_hot = (
        step_flat[:, None] == jnp.arange(time_table.shape[0], dtype=jnp.int32)[None, :]
    ).astype(jnp.float32)
    class_sum = jnp.dot(label_hot.T, all_dcond, precision=highest)
    time_sum = jnp.dot(step_hot.T, all_dcond, precision=highest)
    owned = (
        lax.psum_scatter(class_sum, "fsdp", scatter_dimension=1, tiled=True),
        lax.psum_scatter(time_sum, "fsdp", scatter_dimension=1, tiled=True),
        lax.psum_scatter(totals[0], "fsdp", scatter_dimension=1, tiled=True),
        lax.psum_scatter(totals[1], "fsdp", scatter_dimension=1, tiled=True),
        lax.psum_scatter(totals[2], "fsdp", scatter_dimension=1, tiled=True),
        lax.psum_scatter(totals[3], "fsdp", scatter_dimension=1, tiled=True),
        lax.psum_scatter(totals[4], "fsdp", scatter_dimension=1, tiled=True),
        lax.psum_scatter(totals[5], "fsdp", scatter_dimension=1, tiled=True),
        lax.psum_scatter(totals[6], "fsdp", scatter_dimension=1, tiled=True),
        lax.psum_scatter(totals[7], "fsdp", scatter_dimension=1, tiled=True),
        lax.psum_scatter(totals[8], "fsdp", scatter_dimension=1, tiled=True),
        lax.psum_scatter(totals[9], "fsdp", scatter_dimension=1, tiled=True),
    )
    class_own = owned[0]
    time_own = owned[1]
    block_own = owned[2:]
    summed = (
        lax.psum(class_own.astype(jnp.bfloat16), "rep").astype(jnp.float32),
        lax.psum(time_own.astype(jnp.bfloat16), "rep").astype(jnp.float32),
        lax.psum(block_own[0].astype(jnp.bfloat16), "rep").astype(jnp.float32),
        lax.psum(block_own[1].astype(jnp.bfloat16), "rep").astype(jnp.float32),
        lax.psum(block_own[2].astype(jnp.bfloat16), "rep").astype(jnp.float32),
        lax.psum(block_own[3].astype(jnp.bfloat16), "rep").astype(jnp.float32),
        lax.psum(block_own[4].astype(jnp.bfloat16), "rep").astype(jnp.float32),
        lax.psum(block_own[5].astype(jnp.bfloat16), "rep").astype(jnp.float32),
        lax.psum(block_own[6].astype(jnp.bfloat16), "rep").astype(jnp.float32),
        lax.psum(block_own[7].astype(jnp.bfloat16), "rep").astype(jnp.float32),
        lax.psum(block_own[8].astype(jnp.bfloat16), "rep").astype(jnp.float32),
        lax.psum(block_own[9].astype(jnp.bfloat16), "rep").astype(jnp.float32),
    )
    return (
        jnp.stack(out_list),
        jnp.stack(grad_list),
        summed[0],
        summed[1],
        summed[2],
        summed[3],
        summed[4],
        summed[5],
        summed[6],
        summed[7],
        summed[8],
        summed[9],
        summed[10],
        summed[11],
    )


def solution(mesh):
    in_specs = (
        P(None, ("fsdp", "rep"), None, None),
        P(None, ("fsdp", "rep"), None, None),
        P(None, ("fsdp", "rep")),
        P(None, ("fsdp", "rep")),
        P(None, ("fsdp", "rep")),
        P(None, "fsdp"),
        P(None, "fsdp"),
        P(None, "fsdp", None),
        P(None, "fsdp"),
        P(None, "fsdp", None),
        P(None, "fsdp"),
        P(None, "fsdp", None),
        P(None, "fsdp"),
        P(None, "fsdp", None),
        P(None, "fsdp"),
        P(None, "fsdp", None),
        P(None, "fsdp"),
    )
    out_specs = (
        P(None, ("fsdp", "rep"), None, None),
        P(None, ("fsdp", "rep"), None, None),
        P(None, "fsdp"),
        P(None, "fsdp"),
        P(None, "fsdp", None),
        P(None, "fsdp"),
        P(None, "fsdp", None),
        P(None, "fsdp"),
        P(None, "fsdp", None),
        P(None, "fsdp"),
        P(None, "fsdp", None),
        P(None, "fsdp"),
        P(None, "fsdp", None),
        P(None, "fsdp"),
    )
    return jax.shard_map(
        on_device, mesh=mesh, in_specs=in_specs, out_specs=out_specs, check_vma=False
    )
```

profile of v0, /device:TPU:0, one launch (start us, length us, event | category | flops | bytes accessed | tf_op | source)
XLA Modules:
  0.0 2646.9 jit_solution(17028119992815463005)
XLA Ops:
  10.0 34.6 %all_gather.24 = bf16[1000,384]{0,1:T(8,128)(2,1)S(1)} all-gather(bf16[1000,48]{0,1:T(8,128)(2,1)} %param.48), channel_id=1, replica_groups=mesh['fsdp'=8,'rep'=4] {'fsdp'}, dimensions={1}, use_global_device_ids=true | all-gather | bytes 864000 | tf_op jit(solution)/shard_map/all_gather | solution.py:280
  45.1 33.9 %all_gather.25 = bf16[1000,384]{0,1:T(8,128)(2,1)S(1)} all-gather(bf16[1000,48]{0,1:T(8,128)(2,1)S(1)} %copy-done.438), channel_id=1, replica_groups=mesh['fsdp'=8,'rep'=4] {'fsdp'}, dimensions={1}, use_global_device_ids=true | all-gather | bytes 864000 | tf_op jit(solution)/shard_map/all_gather | solution.py:281
  79.4 26.2 all-gather
  105.7 18.6 all-gather.3
  125.0 16.4 all-gather.1
  141.5 18.3 all-gather.2
  160.5 16.4 all-gather.4
  191.7 35.3 %all_gather.30 = bf16[2,384,384]{2,1,0:T(8,128)(2,1)} all-gather(bf16[2,48,384]{2,1,0:T(8,128)(2,1)} %param.54), channel_id=1, replica_groups=mesh['fsdp'=8,'rep'=4] {'fsdp'}, dimensions={1}, use_global_device_ids=true | all-gather | bytes 663552 | tf_op jit(solution)/shard_map/all_gather | solution.py:286
  229.1 17.4 all-gather.10.cloned.1.call-done
  248.5 38.9 %while.132 = (s32[]{:T(128)}, bf16[2,256,384]{2,1,0:T(8,128)(2,1)}, f32[2,2,256,384]{3,2,1,0:T(8,128)}, pred[2]{0:T(512)(128)(4,1)S(1)}, bf16[2,256,384]{2,1,0:T...) while((s32[]{:T(128)}, bf16[2,256,384]{2,1,0:T(8,128)(2,1)}, ...), condition=%wide.region_15.17_spmd, body=%wide.region_0.16_spmd.sunk | while | flops 2035107840 | bytes 76287800 | solution.py:303
  249.8 32.6 %conditional.12 = (bf16[1,256,384]{2,1,0:T(8,128)(2,1)S(1)}, f32[1,2,256,384]{3,2,1,0:T(8,128)S(1)}) conditional(s32[]{:T(128)} %bitcast.1054, () %tuple.492, (bf16[2,256,384]{2,1,0:T(8,128)(2,1)}, s32[]{:T(128)}, bf16[2,384]{1,0:T(2,128)(2,1)}, bf16[2,384,2304]{2,1,0:T(8,128)(2,1)}, bf16[2,2304]{1,0:T(2,128)(2,1)S(1)}, ...), branch_computations={%region_1.2_spmd, %region_2.15_spmd} | conditional | flops 2035107840 | bytes 71175088 | solution.py:202
  303.5 197.1 %while.135 = (s32[]{:T(128)}, f32[2,384,2304]{2,1,0:T(8,128)}, f32[2,2304]{1,0:T(2,128)}, f32[2,384,1152]{2,1,0:T(8,128)}, f32[2,768]{1,0:T(2,128)}, /*index=5*/...) while((s32[]{:T(128)}, f32[2,384,2304]{2,1,0:T(8,128)}, ...), condition=%wide.region_95.97_spmd, body=%wide.region_48.96_spmd.sunk | while | flops 6146791424 | bytes 465508160 | solution.py:328
  324.4 161.1 %conditional.15 = (f32[2,384,2304]{2,1,0:T(8,128)}, f32[2,2304]{1,0:T(2,128)}, f32[2,384,1152]{2,1,0:T(8,128)}, f32[2,768]{1,0:T(2,128)}, f32[2,384,384]{2,1,0:T...) conditional(s32[]{:T(128)} %bitcast.1057, ...), branch_computations={%region_49.50_spmd, %region_50.95_spmd} | conditional | flops 6146791424 | bytes 465110848 | solution.py:232
  397.6 5.5 maximum_add_fusion.1
  405.4 5.2 maximum_add_fusion.2
  477.8 4.8 maximum_add_fusion
  502.7 69.7 %while.133 = (s32[]{:T(128)}, bf16[2,256,384]{2,1,0:T(8,128)(2,1)}, f32[2,2,256,384]{3,2,1,0:T(8,128)}, pred[2]{0:T(512)(128)(4,1)}, bf16[2,256,384]{2,1,0:T(8,1...) while((s32[]{:T(128)}, bf16[2,256,384]{2,1,0:T(8,128)(2,1)}, ...), condition=%wide.region_31.33_spmd, body=%wide.region_16.32_spmd.sunk | while | flops 2035107840 | bytes 69982512 | solution.py:303
  504.6 56.9 %conditional.13 = (bf16[1,256,384]{2,1,0:T(8,128)(2,1)}, f32[1,2,256,384]{3,2,1,0:T(8,128)}) conditional(s32[]{:T(128)} %bitcast.1055, () %tuple.495, (bf16[2,256,384]{2,1,0:T(8,128)(2,1)}, s32[]{:T(128)}, bf16[2,384]{1,0:T(2,128)(2,1)}, bf16[2,384,2304]{2,1,0:T(8,128)(2,1)S(1)}, bf16[2,2304]{1,0:T(2,128)(2,1)S(1)}, ...), branch_computations={%region_17.18_spmd, %region_18.31_spmd} | conditional | flops 2035107840 | bytes 68015136 | solution.py:202
  573.8 196.1 %while.136 = (s32[]{:T(128)}, f32[2,384,2304]{2,1,0:T(8,128)}, f32[2,2304]{1,0:T(2,128)}, f32[2,384,1152]{2,1,0:T(8,128)}, f32[2,768]{1,0:T(2,128)}, /*index=5*/...) while((s32[]{:T(128)}, f32[2,384,2304]{2,1,0:T(8,128)}, ...), condition=%wide.region_143.145_spmd, body=%wide.region_96.144_spmd.sunk | while | flops 6146791424 | bytes 465520512 | solution.py:328
  594.7 160.1 %conditional.16 = (f32[2,384,2304]{2,1,0:T(8,128)}, f32[2,2304]{1,0:T(2,128)}, f32[2,384,1152]{2,1,0:T(8,128)}, f32[2,768]{1,0:T(2,128)}, f32[2,384,384]{2,1,0:T...) conditional(s32[]{:T(128)} %bitcast.1058, ...), branch_computations={%region_97.98_spmd, %region_98.143_spmd} | conditional | flops 6146791424 | bytes 465123200 | solution.py:232
  667.5 5.5 maximum_add_fusion.11
  675.3 5.2 maximum_add_fusion.12
  747.0 4.8 maximum_add_fusion.10
  771.9 125.0 %while.134 = (s32[]{:T(128)}, bf16[2,256,384]{2,1,0:T(8,128)(2,1)}, f32[2,2,256,384]{3,2,1,0:T(8,128)}, pred[2]{0:T(512)(128)(4,1)}, bf16[2,256,384]{2,1,0:T(8,1...) while((s32[]{:T(128)}, bf16[2,256,384]{2,1,0:T(8,128)(2,1)}, ...), condition=%wide.region_47.49_spmd, body=%wide.region_32.48_spmd.sunk | while | flops 2035107840 | bytes 69982512 | solution.py:303
  773.7 57.0 %conditional.14 = (bf16[1,256,384]{2,1,0:T(8,128)(2,1)}, f32[1,2,256,384]{3,2,1,0:T(8,128)}) conditional(s32[]{:T(128)} %bitcast.1056, () %tuple.498, (bf16[2,256,384]{2,1,0:T(8,128)(2,1)}, s32[]{:T(128)}, bf16[2,384]{1,0:T(2,128)(2,1)}, bf16[2,384,2304]{2,1,0:T(8,128)(2,1)S(1)}, bf16[2,2304]{1,0:T(2,128)(2,1)S(1)}, ...), branch_computations={%region_33.34_spmd, %region_34.47_spmd} | conditional | flops 2035107840 | bytes 68015136 | solution.py:202
  836.2 57.0 %conditional.14 = (bf16[1,256,384]{2,1,0:T(8,128)(2,1)}, f32[1,2,256,384]{3,2,1,0:T(8,128)}) conditional(s32[]{:T(128)} %bitcast.1056, () %tuple.498, (bf16[2,256,384]{2,1,0:T(8,128)(2,1)}, s32[]{:T(128)}, bf16[2,384]{1,0:T(2,128)(2,1)}, bf16[2,384,2304]{2,1,0:T(8,128)(2,1)S(1)}, bf16[2,2304]{1,0:T(2,128)(2,1)S(1)}, ...), branch_computations={%region_33.34_spmd, %region_34.47_spmd} | conditional | flops 2035107840 | bytes 68015136 | solution.py:202
  898.3 348.5 %while.137 = (s32[]{:T(128)}, f32[2,384,2304]{2,1,0:T(8,128)}, f32[2,2304]{1,0:T(2,128)}, f32[2,384,1152]{2,1,0:T(8,128)}, f32[2,768]{1,0:T(2,128)}, /*index=5*/...) while((s32[]{:T(128)}, f32[2,384,2304]{2,1,0:T(8,128)}, ...), condition=%wide.region_191.193_spmd, body=%wide.region_144.192_spmd.sunk | while | flops 6146791424 | bytes 465520512 | solution.py:328
  919.1 159.9 %conditional.17 = (f32[2,384,2304]{2,1,0:T(8,128)}, f32[2,2304]{1,0:T(2,128)}, f32[2,384,1152]{2,1,0:T(8,128)}, f32[2,768]{1,0:T(2,128)}, f32[2,384,384]{2,1,0:T...) conditional(s32[]{:T(128)} %bitcast.1059, ...), branch_computations={%region_145.146_spmd, %region_146.191_spmd} | conditional | flops 6146791424 | bytes 465123200 | solution.py:232
  991.8 5.5 maximum_add_fusion.21
  999.6 5.2 maximum_add_fusion.22
  1071.3 4.8 maximum_add_fusion.20
  1083.7 159.9 %conditional.17 = (f32[2,384,2304]{2,1,0:T(8,128)}, f32[2,2304]{1,0:T(2,128)}, f32[2,384,1152]{2,1,0:T(8,128)}, f32[2,768]{1,0:T(2,128)}, f32[2,384,384]{2,1,0:T...) conditional(s32[]{:T(128)} %bitcast.1059, ...), branch_computations={%region_145.146_spmd, %region_146.191_spmd} | conditional | flops 6146791424 | bytes 465123200 | solution.py:232
  1156.5 5.5 maximum_add_fusion.21
  1164.2 5.2 maximum_add_fusion.22
  1261.4 454.5 %reduce-scatter.31.cloned.1.call-done = f32[2,48,384]{2,1,0:T(8,128)} async-done(((f32[2,384,384]{2,1,0:T(8,128)}), f32[2,48,384]{2,1,0:T(8,128)}) %reduce-scatter.31.cloned.1.call-update) | async-done | bytes 147472 | tf_op jit(solution)/shard_map/reduce_scatter | solution.py:351
  1717.4 65.6 %reduce-scatter.25.cloned.1.call-done = f32[1000,48]{0,1:T(8,128)} async-done(((f32[1000,384]{0,1:T(8,128)}), f32[1000,48]{0,1:T(8,128)}) %reduce-scatter.25.cloned.1.call-update) | async-done | bytes 192016 | tf_op jit(solution)/shard_map/reduce_scatter | solution.py:346
  1784.5 66.0 %reduce-scatter.23.cloned.1.call-done = f32[1000,48]{0,1:T(8,128)} async-done(((f32[1000,384]{0,1:T(8,128)}), f32[1000,48]{0,1:T(8,128)}) %reduce-scatter.23.cloned.1.call-update) | async-done | bytes 192016 | tf_op jit(solution)/shard_map/reduce_scatter | solution.py:345
  1852.1 80.2 %reduce-scatter.29.cloned.1.call-done = f32[2,48,1152]{2,1,0:T(8,128)} async-done(((f32[2,384,1152]{2,1,0:T(8,128)}), f32[2,48,1152]{2,1,0:T(8,128)}) %reduce-scatter.29.cloned.1.call-update) | async-done | bytes 442384 | tf_op jit(solution)/shard_map/reduce_scatter | solution.py:349
  1934.0 96.7 %reduce-scatter.33.cloned.1.call-done = f32[2,48,1536]{2,1,0:T(8,128)} async-done(((f32[2,384,1536]{2,1,0:T(8,128)}), f32[2,48,1536]{2,1,0:T(8,128)}) %reduce-scatter.33.cloned.1.call-update) | async-done | bytes 589840 | tf_op jit(solution)/shard_map/reduce_scatter | solution.py:353
  2032.6 96.7 %reduce-scatter.35.cloned.1.call-done = f32[2,192,384]{2,1,0:T(8,128)} async-done(((f32[2,1536,384]{2,1,0:T(8,128)}), f32[2,192,384]{2,1,0:T(8,128)}) %reduce-scatter.35.cloned.1.call-update) | async-done | bytes 589840 | tf_op jit(solution)/shard_map/reduce_scatter | solution.py:355
  2131.1 131.1 %reduce-scatter.27.cloned.1.call-done = f32[2,48,2304]{2,1,0:T(8,128)} async-done(((f32[2,384,2304]{2,1,0:T(8,128)}), f32[2,48,2304]{2,1,0:T(8,128)}) %reduce-scatter.27.cloned.1.call-update) | async-done | bytes 884752 | tf_op jit(solution)/shard_map/reduce_scatter | solution.py:347
  2267.7 58.6 %reduce-scatter.41.cloned.1.call-done = f32[48,2]{1,0:T(8,128)} async-done(((f32[384,2]{1,0:T(8,128)}), f32[48,2]{1,0:T(8,128)}) %reduce-scatter.41.cloned.1.call-update) | async-done | bytes 400
  2327.1 63.5 %reduce-scatter.45.cloned.1.call-done = f32[48,2]{1,0:T(8,128)} async-done(((f32[384,2]{1,0:T(8,128)}), f32[48,2]{1,0:T(8,128)}) %reduce-scatter.45.cloned.1.call-update) | async-done | bytes 400
  2391.4 63.1 %reduce-scatter.39.cloned.1.call-done = f32[96,2]{1,0:T(8,128)} async-done(((f32[768,2]{1,0:T(8,128)}), f32[96,2]{1,0:T(8,128)}) %reduce-scatter.39.cloned.1.call-update) | async-done | bytes 784
  2455.4 64.8 %reduce-scatter.43.cloned.1.call-done = f32[192,2]{1,0:T(8,128)} async-done(((f32[1536,2]{1,0:T(8,128)}), f32[192,2]{1,0:T(8,128)}) %reduce-scatter.43.cloned.1.call-update) | async-done | bytes 1552
  2521.1 65.2 %reduce-scatter.37.cloned.1.call-done = f32[288,2]{1,0:T(8,128)} async-done(((f32[2304,2]{1,0:T(8,128)}), f32[288,2]{1,0:T(8,128)}) %reduce-scatter.37.cloned.1.call-update) | async-done | bytes 2320
  2587.3 5.7 all-reduce
  2595.8 36.7 %all-reduce.4.cloned.1.call-done = (bf16[1000,48]{0,1:T(8,128)(2,1)}, bf16[1000,48]{0,1:T(8,128)(2,1)}, bf16[2,48,2304]{2,1,0:T(8,128)(2,1)}, bf16[2,48,1152]{2,...) async-done(((bf16[1000,48]{0,1:T(8,128)(2,1)}, bf16[1000,48]{0,1:T(8,128)(2,1)}, ...) | async-done | bytes 1519120 | tf_op jit(solution)/shard_map/psum | solution.py:362
  (2169 shorter events, 929.9 us)
Async XLA Ops:
  7.2 222.0 %all-gather.12.cloned.1.call-start = ((), (), s32[]{:S(2)}) async-start(), calls=%async_computation.13 | async-start | bytes 1990656 | tf_op jit(solution)/shard_map/all_gather | solution.py:284
  7.9 221.2 %all-gather.14.cloned.1.call-start = ((), (), s32[]{:S(2)}) async-start(), calls=%async_computation.14 | async-start | bytes 2654208 | tf_op jit(solution)/shard_map/all_gather | solution.py:288
  8.7 36.4 %copy-start.438 = (bf16[1000,48]{0,1:T(8,128)(2,1)S(1)}, bf16[1000,48]{0,1:T(8,128)(2,1)}, u32[]{:S(2)}) copy-start(bf16[1000,48]{0,1:T(8,128)(2,1)} %param.49) | copy-start | bytes 288004
  8.7 220.5 %all-gather.16.cloned.1.call-start = ((), (), s32[]{:S(2)}) async-start(), calls=%async_computation.15 | async-start | bytes 2654208 | tf_op jit(solution)/shard_map/all_gather | solution.py:290
  9.4 237.1 %all-gather.10.cloned.1.call-start = ((), (), s32[]{:S(2)}) async-start(), calls=%async_computation.12 | async-start | bytes 3981312 | tf_op jit(solution)/shard_map/all_gather | solution.py:282
  10.0 1705.9 %reduce-scatter.31.cloned.1.call-start = ((), (), s32[]{:S(2)}) async-start(), calls=%async_computation.20 | async-start | bytes 1327104 | tf_op jit(solution)/shard_map/reduce_scatter | solution.py:351
  45.0 134.7 %copy-start.256 = (bf16[1000,384]{1,0:T(8,128)(2,1)}, bf16[1000,384]{1,0:T(8,128)(2,1)S(1)}, u32[]{:S(2)}) copy-start(bf16[1000,384]{1,0:T(8,128)(2,1)S(1)} %copy.369) | copy-start | bytes 2304004
  45.0 34.4 %copy-start.454 = (bf16[2,288]{1,0:T(2,128)(2,1)S(1)}, bf16[2,288]{1,0:T(2,128)(2,1)}, u32[]{:S(2)}) copy-start(bf16[2,288]{1,0:T(2,128)(2,1)} %param.51) | copy-start | bytes 3460
  45.1 60.6 %copy-start.455 = (bf16[2,192]{1,0:T(2,128)(2,1)S(1)}, bf16[2,192]{1,0:T(2,128)(2,1)}, u32[]{:S(2)}) copy-start(bf16[2,192]{1,0:T(2,128)(2,1)} %param.57) | copy-start | bytes 2308
  45.1 132.6 %copy-start.452 = (s32[3,2]{0,1:T(2,128)S(1)}, s32[3,2]{0,1:T(2,128)}, u32[]{:S(2)}) copy-start(s32[3,2]{0,1:T(2,128)} %param.46) | copy-start | bytes 76
  45.1 133.9 %copy-start.451 = (s32[3,2]{0,1:T(2,128)S(1)}, s32[3,2]{0,1:T(2,128)}, u32[]{:S(2)}) copy-start(s32[3,2]{0,1:T(2,128)} %param.47) | copy-start | bytes 76
  45.1 181.9 %copy-start.247 = (bf16[3,2,256,384]{3,2,1,0:T(8,128)(2,1)S(1)}, bf16[3,2,256,384]{3,2,1,0:T(8,128)(2,1)}, u32[]{:S(2)}) copy-start(bf16[3,2,256,384]{3,2,1,0:T(8,128)(2,1)} %param.43) | copy-start | bytes 3538948
  79.4 100.4 %copy-start.255 = (bf16[1000,384]{1,0:T(8,128)(2,1)}, bf16[1000,384]{1,0:T(8,128)(2,1)S(1)}, u32[]{:S(2)}) copy-start(bf16[1000,384]{1,0:T(8,128)(2,1)S(1)} %copy.370) | copy-start | bytes 2304004
  179.8 48.3 %copy-start.248 = (bf16[3,2,256,384]{3,2,1,0:T(8,128)(2,1)S(1)}, bf16[3,2,256,384]{3,2,1,0:T(8,128)(2,1)}, u32[]{:S(2)}) copy-start(bf16[3,2,256,384]{3,2,1,0:T(8,128)(2,1)} %param.44) | copy-start | bytes 3538948
  390.8 12.4 copy-start.105
  441.8 15.3 copy-start.83
  441.8 15.3 copy-start.158
  441.8 15.6 copy-start.89
  441.8 15.6 copy-start.152
  711.8 15.3 copy-start.85
  711.8 15.3 copy-start.160
  711.8 15.5 copy-start.91
  711.8 15.6 copy-start.154
  985.0 12.4 copy-start.109
  1036.0 15.3 copy-start.87
  1036.0 15.3 copy-start.162
  1036.0 15.6 copy-start.93
  1036.0 15.6 copy-start.156
  1149.6 12.4 copy-start.109
  1200.7 15.3 copy-start.87
  1200.7 15.3 copy-start.162
  1200.7 15.6 copy-start.93
  1200.7 15.6 copy-start.156
  1246.8 536.1 %reduce-scatter.25.cloned.1.call-start = ((), (), s32[]{:S(2)}) async-start(), calls=%async_computation.17 | async-start | bytes 1769472 | tf_op jit(solution)/shard_map/reduce_scatter | solution.py:346
  1250.5 600.0 %reduce-scatter.23.cloned.1.call-start = ((), (), s32[]{:S(2)}) async-start(), calls=%async_computation.16 | async-start | bytes 1769472 | tf_op jit(solution)/shard_map/reduce_scatter | solution.py:345
  1252.9 679.4 %reduce-scatter.29.cloned.1.call-start = ((), (), s32[]{:S(2)}) async-start(), calls=%async_computation.19 | async-start | bytes 3981312 | tf_op jit(solution)/shard_map/reduce_scatter | solution.py:349
  1253.6 777.1 %reduce-scatter.33.cloned.1.call-start = ((), (), s32[]{:S(2)}) async-start(), calls=%async_computation.21 | async-start | bytes 5308416 | tf_op jit(solution)/shard_map/reduce_scatter | solution.py:353
  1254.3 874.9 %reduce-scatter.35.cloned.1.call-start = ((), (), s32[]{:S(2)}) async-start(), calls=%async_computation.22 | async-start | bytes 5308416 | tf_op jit(solution)/shard_map/reduce_scatter | solution.py:355
  1254.9 1007.2 %reduce-scatter.27.cloned.1.call-start = ((), (), s32[]{:S(2)}) async-start(), calls=%async_computation.18 | async-start | bytes 7962624 | tf_op jit(solution)/shard_map/reduce_scatter | solution.py:347
  1255.7 1070.6 %reduce-scatter.41.cloned.1.call-start = ((), (), s32[]{:S(2)}) async-start(), calls=%async_computation.25 | async-start | bytes 221184
  1256.6 1134.0 %reduce-scatter.45.cloned.1.call-start = ((), (), s32[]{:S(2)}) async-start(), calls=%async_computation.27 | async-start | bytes 221184
  1257.5 1197.0 %reduce-scatter.39.cloned.1.call-start = ((), (), s32[]{:S(2)}) async-start(), calls=%async_computation.24 | async-start | bytes 442368
  1258.5 1261.6 %reduce-scatter.43.cloned.1.call-start = ((), (), s32[]{:S(2)}) async-start(), calls=%async_computation.26 | async-start | bytes 884736
  1259.8 1326.5 %reduce-scatter.37.cloned.1.call-start = ((), (), s32[]{:S(2)}) async-start(), calls=%async_computation.23 | async-start | bytes 1327104
  1261.3 1371.2 %all-reduce.4.cloned.1.call-start = ((), (), s32[]{:S(2)}) async-start(), calls=%async_computation.28 | async-start | bytes 3047424 | tf_op jit(solution)/shard_map/psum | solution.py:362
  2131.1 133.1 %copy-start.235 = (bf16[2,256,384]{2,1,0:T(8,128)(2,1)S(1)}, bf16[2,256,384]{2,1,0:T(8,128)(2,1)}, u32[]{:S(2)}) copy-start(bf16[2,256,384]{2,1,0:T(8,128)(2,1)} %get-tuple-element.1795) | copy-start | bytes 1179652
  2131.1 133.1 %copy-start.236 = (bf16[2,256,384]{2,1,0:T(8,128)(2,1)S(1)}, bf16[2,256,384]{2,1,0:T(8,128)(2,1)}, u32[]{:S(2)}) copy-start(bf16[2,256,384]{2,1,0:T(8,128)(2,1)} %get-tuple-element.1771) | copy-start | bytes 1179652
  2131.1 133.1 %copy-start.237 = (bf16[2,256,384]{2,1,0:T(8,128)(2,1)S(1)}, bf16[2,256,384]{2,1,0:T(8,128)(2,1)}, u32[]{:S(2)}) copy-start(bf16[2,256,384]{2,1,0:T(8,128)(2,1)} %get-tuple-element.1783) | copy-start | bytes 1179652
  (596 other events, 1490.4 us)
Sparse Core Ops, SparseCore 0:
  10.3 60.1 all-gather.11
  72.6 51.3 all-gather.13
  126.2 51.8 all-gather.15
  180.2 66.3 all-gather.9
  1246.9 468.8 reduce-scatter.30
  1719.1 63.7 reduce-scatter.24
  1786.8 63.7 reduce-scatter.22
  1854.1 78.0 reduce-scatter.28
  1935.9 94.7 reduce-scatter.32
  2034.2 94.9 reduce-scatter.34
  2133.0 129.1 reduce-scatter.26
  2266.2 60.0 reduce-scatter.40
  2330.5 60.0 reduce-scatter.44
  2394.1 60.3 reduce-scatter.38
  2458.6 61.5 reduce-scatter.42
  2523.4 62.8 reduce-scatter.36
  2590.2 42.3 all-reduce.3
where the time goes:
time: 2670 us; the launch traced here: 2650 us
  waiting for transfers between devices  1370 us (51%)
  local copies, waits for them, and re-layouts  386 us (14%)
  matrix products  324 us (12%)
  other arithmetic  267 us (10%)
  blocking collectives  205 us (8%)
  loops' own time  84 us (3%)
    reduce_scatter x1, waiting for transfers between devices, on_device(): lax.psum_scatter(totals[4], 'fsdp', scatter_dimension=1, tiled=True)  454 us
    unnamed x22, waiting for transfers between devices  320 us
    reduce_scatter x1, waiting for transfers between devices, on_device(): lax.psum_scatter(totals[0], 'fsdp', scatter_dimension=1, tiled=True)  131 us
    cond x1220, local copies, waits for them, and re-layouts  123 us
    reduce_scatter x1, waiting for transfers between devices, on_device(): lax.psum_scatter(totals[6], 'fsdp', scatter_dimension=1, tiled=True)  96.7 us
    reduce_scatter x1, waiting for transfers between devices, on_device(): lax.psum_scatter(totals[8], 'fsdp', scatter_dimension=1, tiled=True)  96.7 us
    add x36, other arithmetic, backward_run_slot(): earlier + addition  85.4 us
    reduce_scatter x1, waiting for transfers between devices, on_device(): lax.psum_scatter(totals[2], 'fsdp', scatter_dimension=1, tiled=True)  80.2 us
  transfers between devices with their start and end apart: 17, of which 14 were waited for; matrix products, arithmetic and copies ran while one was open for 2% of the time, Pallas kernels for 0%

commit v1 on v0

v1 whole, which is shorter than its diff:
```python
from functools import partial

import jax
import jax.numpy as jnp
from jax import lax
from jax.experimental import pallas as pl
from jax.experimental.pallas import tpu as pltpu
from jax.sharding import PartitionSpec as P

HEADS = 6
LAYERS = 2
EPS = 1e-06
GELU_C = 0.7978845608028654
GELU_A = 0.044715
F32 = jnp.float32
BF16 = jnp.bfloat16


def dot(a, b, dims=((1,), (0,))):
    return lax.dot_general(a, b, (dims, ((), ())), preferred_element_type=F32)


def dot_nt(a, b):
    return dot(a, b, ((1,), (1,)))


def dot_tn(a, b):
    return dot(a, b, ((0,), (0,)))


def norm(x):
    centred = x - jnp.mean(x, axis=-1, keepdims=True)
    inv = lax.rsqrt(jnp.mean(centred * centred, axis=-1, keepdims=True) + EPS)
    return centred * inv, inv


def norm_back(n, inv, dn):
    return inv * (
        dn - jnp.mean(dn, axis=-1, keepdims=True) - n * jnp.mean(dn * n, axis=-1, keepdims=True)
    )


def col_sum(x):
    return jnp.sum(x, axis=0, keepdims=True)


def fwd_kernel(last, d, ff, live_ref, r_ref, mod_ref, wa_ref, wf2_ref, bias_ref,
               out_ref, qkv_ref, blend_ref, branch_ref, mid_ref, hin_ref, mlp_ref):
    mod = mod_ref[0]
    sh_a, sc_a, g_a, sh_m, sc_m, g_m = [mod[i : i + 1] for i in range(6)]
    hd = d // HEADS
    r = r_ref[0].astype(F32)
    n_a, _ = norm(r)
    moved = (n_a * (1.0 + sc_a) + sh_a).astype(BF16)
    q = dot(moved, wa_ref[:, :d]) + bias_ref[:, :d]
    k = dot(moved, wa_ref[:, d : 2 * d])
    v = dot(moved, wa_ref[:, 2 * d : 3 * d]) + bias_ref[:, d : 2 * d]
    q = q.astype(BF16)
    k = k.astype(BF16)
    v = v.astype(BF16)
    qkv_ref[0, :, :d] = q
    qkv_ref[0, :, d : 2 * d] = k
    qkv_ref[0, :, 2 * d :] = v
    qs = q * jnp.asarray(hd**-0.5, BF16)
    parts = []
    for h in range(HEADS):
        c = slice(h * hd, (h + 1) * hd)
        s = dot_nt(qs[:, c], k[:, c])
        e = jnp.exp(s - jnp.max(s, axis=-1, keepdims=True))
        inv = 1.0 / jnp.sum(e, axis=-1, keepdims=True)
        parts.append((dot(e.astype(BF16), v[:, c]) * inv).astype(BF16))
    blend = jnp.concatenate(parts, axis=1)
    blend_ref[0] = blend
    branch = dot(blend, wa_ref[:, 3 * d : 4 * d]) + bias_ref[:, 2 * d : 3 * d]
    branch_ref[0] = branch.astype(BF16)
    mid = r + g_a * branch
    mid_ref[0] = mid
    n_m, _ = norm(mid)
    moved = (n_m * (1.0 + sc_m) + sh_m).astype(BF16)
    hin = dot(moved, wa_ref[:, 4 * d :]) + bias_ref[:, 3 * d : 3 * d + ff]
    hin_ref[0] = hin.astype(BF16)
    t = jnp.tanh(GELU_C * (hin + GELU_A * hin * hin * hin))
    hidden = (0.5 * hin * (1.0 + t)).astype(BF16)
    mlp = dot(hidden, wf2_ref[...]) + bias_ref[:, 3 * d + ff :]
    mlp_ref[0] = mlp.astype(BF16)
    out = mid + g_m * mlp
    if last:
        out = jnp.where(live_ref[pl.program_id(0)] > 0, out, 0.0)
    out_ref[0] = out.astype(out_ref.dtype)


def bwd_kernel(first, last, d, ff, live_ref, g_ref, r_ref, mod_ref, wa_ref, wf2_ref,
               qkv_ref, blend_ref, branch_ref, mid_ref, hin_ref, mlp_ref,
               dr_ref, dmod_ref, dwa_ref, dwf2_ref, dbias_ref, acc_a, acc_f2):
    step = pl.program_id(0)

    @pl.when(step == 0)
    def _():
        acc_a[...] = jnp.zeros_like(acc_a)
        acc_f2[...] = jnp.zeros_like(acc_f2)
        dbias_ref[...] = jnp.zeros_like(dbias_ref)

    mod = mod_ref[0]
    _, sc_a, g_a, _, sc_m, g_m = [mod[i : i + 1] for i in range(6)]
    hd = d // HEADS
    g = g_ref[0].astype(F32)
    if last:
        g = jnp.where(live_ref[step] > 0, g, 0.0)
    dgm = col_sum(g * mlp_ref[0].astype(F32))
    gmlp_f = g_m * g
    dbias_ref[:, 3 * d + ff :] += col_sum(gmlp_f)
    gmlp = gmlp_f.astype(BF16)
    hin = hin_ref[0].astype(F32)
    sq = hin * hin
    t = jnp.tanh(GELU_C * hin * (1.0 + GELU_A * sq))
    half = 0.5 * (1.0 + t)
    hidden = (hin * half).astype(BF16)
    acc_f2[...] += dot_tn(hidden, gmlp)
    slope = half + (0.5 * GELU_C) * hin * (1.0 - t * t) * (1.0 + (3.0 * GELU_A) * sq)
    ghin_f = dot_nt(gmlp, wf2_ref[...]) * slope
    dbias_ref[:, 3 * d : 3 * d + ff] += col_sum(ghin_f)
    ghin = ghin_f.astype(BF16)
    n_m, inv_m = norm(mid_ref[0])
    mod_m = mod[3:4]
    moved = (n_m * (1.0 + sc_m) + mod_m).astype(BF16)
    acc_a[:, 4 * d :] += dot_tn(moved, ghin)
    gmoved = dot_nt(ghin, wa_ref[:, 4 * d :])
    dshm = col_sum(gmoved)
    dscm = col_sum(gmoved * n_m)
    gmid = g + norm_back(n_m, inv_m, gmoved * (1.0 + sc_m))
    dga = col_sum(gmid * branch_ref[0].astype(F32))
    gbr_f = g_a * gmid
    dbias_ref[:, 2 * d : 3 * d] += col_sum(gbr_f)
    gbr = gbr_f.astype(BF16)
    blend = blend_ref[0]
    acc_a[:, 3 * d : 4 * d] += dot_tn(blend, gbr)
    gbl = dot_nt(gbr, wa_ref[:, 3 * d : 4 * d]).astype(BF16)
    prod = gbl.astype(F32) * blend.astype(F32)
    q = qkv_ref[0, :, :d] * jnp.asarray(hd**-0.5, BF16)
    k = qkv_ref[0, :, d : 2 * d]
    v = qkv_ref[0, :, 2 * d :]
    dq, dk, dv = [], [], []
    for h in range(HEADS):
        c = slice(h * hd, (h + 1) * hd)
        s = dot_nt(q[:, c], k[:, c])
        e = jnp.exp(s - jnp.max(s, axis=-1, keepdims=True))
        soft = e * (1.0 / jnp.sum(e, axis=-1, keepdims=True))
        gs = dot_nt(gbl[:, c], v[:, c])
        dv.append(dot_tn(soft.astype(BF16), gbl[:, c]))
        ds = (soft * (gs - jnp.sum(prod[:, c], axis=-1, keepdims=True))).astype(BF16)
        dq.append(dot(ds, k[:, c]) * (hd**-0.5))
        dk.append(dot_tn(ds, q[:, c]))
    dq = jnp.concatenate(dq, axis=1)
    dk = jnp.concatenate(dk, axis=1)
    dv = jnp.concatenate(dv, axis=1)
    dbias_ref[:, :d] += col_sum(dq)
    dbias_ref[:, d : 2 * d] += col_sum(dv)
    dqkv = jnp.concatenate([dq, dk, dv], axis=1).astype(BF16)
    n_a, inv_a = norm(r_ref[0].astype(F32))
    moved = (n_a * (1.0 + sc_a) + mod[0:1]).astype(BF16)
    acc_a[:, : 3 * d] += dot_tn(moved, dqkv)
    gmoved = dot_nt(dqkv, wa_ref[:, : 3 * d])
    dsha = col_sum(gmoved)
    dsca = col_sum(gmoved * n_a)
    dr = gmid + norm_back(n_a, inv_a, gmoved * (1.0 + sc_a))
    dr_ref[0] = dr.astype(dr_ref.dtype)
    dmod_ref[0] = jnp.concatenate([dsha, dsca, dga, dshm, dscm, dgm], axis=0)

    @pl.when(step == pl.num_programs(0) - 1)
    def _():
        dwa_ref[...] = acc_a[...].astype(BF16)
        dwf2_ref[...] = acc_f2[...].astype(BF16)


def row_spec(*shape):
    return pl.BlockSpec((1,) + shape, lambda i: (i, 0, 0))


def full_spec(*shape):
    return pl.BlockSpec(shape, lambda i: (0,) * len(shape))


SMEM = pl.BlockSpec(memory_space=pltpu.SMEM)
PARAMS = pltpu.CompilerParams(
    dimension_semantics=("arbitrary",), vmem_limit_bytes=56 * 1024 * 1024
)


def layer_forward(last, live, r, mod, wa, wf2, bias):
    n, length, d = r.shape
    ff = wf2.shape[0]
    sds = jax.ShapeDtypeStruct
    return pl.pallas_call(
        partial(fwd_kernel, last, d, ff),
        grid=(n,),
        in_specs=[SMEM, row_spec(length, d), row_spec(6, d), full_spec(*wa.shape),
                  full_spec(*wf2.shape), full_spec(*bias.shape)],
        out_specs=[row_spec(length, d), row_spec(length, 3 * d), row_spec(length, d),
                   row_spec(length, d), row_spec(length, d), row_spec(length, ff),
                   row_spec(length, d)],
        out_shape=[
            sds((n, length, d), BF16 if last else F32),
            sds((n, length, 3 * d), BF16),
            sds((n, length, d), BF16),
            sds((n, length, d), BF16),
            sds((n, length, d), F32),
            sds((n, length, ff), BF16),
            sds((n, length, d), BF16),
        ],
        compiler_params=PARAMS,
        name="layer_forward",
    )(live, r, mod, wa, wf2, bias)


def layer_backward(first, last, live, g, r, mod, wa, wf2, saved):
    n, length, d = r.shape
    ff = wf2.shape[0]
    sds = jax.ShapeDtypeStruct
    width = 4 * d + ff
    return pl.pallas_call(
        partial(bwd_kernel, first, last, d, ff),
        grid=(n,),
        in_specs=[SMEM, row_spec(length, d), row_spec(length, d), row_spec(6, d),
                  full_spec(*wa.shape), full_spec(*wf2.shape), row_spec(length, 3 * d),
                  row_spec(length, d), row_spec(length, d), row_spec(length, d),
                  row_spec(length, ff), row_spec(length, d)],
        out_specs=[row_spec(length, d), row_spec(6, d), full_spec(d, width), full_spec(ff, d),
                   full_spec(1, 4 * d + ff)],
        out_shape=[
            sds((n, length, d), BF16 if first else F32),
            sds((n, 6, d), F32),
            sds((d, width), BF16),
            sds((ff, d), BF16),
            sds((1, 4 * d + ff), F32),
        ],
        scratch_shapes=[pltpu.VMEM((d, width), F32), pltpu.VMEM((ff, d), F32)],
        compiler_params=PARAMS,
        name="layer_backward",
    )(live, g, r, mod, wa, wf2, *saved)


def on_device(latents, cotangent, counts, labels, timesteps, class_table, time_table,
              ada_weight, ada_bias, qkv_weight, qv_bias, proj_weight, proj_bias,
              fc1_weight, fc1_bias, fc2_weight, fc2_bias):
    micro, slots, length, d = latents.shape
    n = micro * slots
    ff = fc1_weight.shape[2]
    owners = lax.axis_size("fsdp")
    me = lax.axis_index("fsdp")

    biases = (ada_bias, qv_bias, proj_bias, fc1_bias, fc2_bias)
    head = jnp.concatenate(
        [x.astype(F32).reshape(-1) for x in (labels, timesteps) + biases]
    )
    head = lax.all_gather(head, "fsdp")
    wa = []
    wf2 = []
    for l in range(LAYERS):
        packed = jnp.concatenate([qkv_weight[l], proj_weight[l], fc1_weight[l]], axis=1)
        wa.append(lax.all_gather(packed, "fsdp", axis=0, tiled=True))
        wf2.append(lax.all_gather(fc2_weight[l], "fsdp", axis=0, tiled=True))

    full_bias = []
    at = 2 * n
    for b in biases:
        w = b.shape[1]
        got = head[:, at : at + LAYERS * w].reshape(owners, LAYERS, w)
        full_bias.append(jnp.moveaxis(got, 0, 1).reshape(LAYERS, owners * w))
        at += LAYERS * w
    ada_b = full_bias[0]
    layer_bias = jnp.concatenate(full_bias[1:], axis=1)

    classes = class_table.shape[0]
    steps = time_table.shape[0]
    all_labels = head[:, :n].reshape(-1).astype(jnp.int32)
    all_steps = head[:, n : 2 * n].reshape(-1).astype(jnp.int32)
    label_hot = all_labels[:, None] == jnp.arange(classes, dtype=jnp.int32)[None, :]
    step_hot = all_steps[:, None] == jnp.arange(steps, dtype=jnp.int32)[None, :]
    cond = dot(label_hot.astype(BF16), class_table) + dot(step_hot.astype(BF16), time_table)
    sig = jax.nn.sigmoid(cond)
    lifted = (cond * sig).astype(BF16)
    part = jnp.concatenate([dot(lifted, ada_weight[l]) for l in range(LAYERS)], axis=1)
    mod = lax.psum_scatter(part, "fsdp", scatter_dimension=0, tiled=True)
    mod = mod.reshape(n, LAYERS, 6 * d) + ada_b[None]
    mod = [mod[:, l].reshape(n, 6, d) for l in range(LAYERS)]

    slot_ids = jnp.arange(slots, dtype=jnp.int32)
    live = (slot_ids[None, :] < counts).astype(jnp.int32).reshape(-1)

    r = latents.reshape(n, length, d)
    ins, saved = [], []
    for l in range(LAYERS):
        ins.append(r)
        r, *rest = layer_forward(
            l == LAYERS - 1, live, r, mod[l], wa[l], wf2[l], layer_bias[l][None]
        )
        saved.append(rest)
    outputs = r.reshape(latents.shape)

    g = cotangent.reshape(n, length, d)
    grads = [None] * LAYERS
    sums = [None] * LAYERS
    tails = [None] * LAYERS
    lift_grad = jnp.zeros(cond.shape, F32)
    for l in reversed(range(LAYERS)):
        g, dmod, dwa, dwf2, dbias = layer_backward(
            l == 0, l == LAYERS - 1, live, g, ins[l], mod[l], wa[l], wf2[l], saved[l]
        )
        dwa = lax.psum_scatter(dwa, "rep", scatter_dimension=1, tiled=True)
        dwa = lax.psum_scatter(dwa, "fsdp", scatter_dimension=0, tiled=True)
        dwf2 = dwf2.reshape(owners, ff // owners, d)
        dwf2 = lax.psum_scatter(dwf2, "rep", scatter_dimension=1, tiled=True)
        dwf2 = lax.psum_scatter(dwf2, "fsdp", scatter_dimension=0, tiled=True)[0]
        sums[l] = (dwa, dwf2)
        tails[l] = jnp.concatenate([dmod.reshape(-1), dbias.reshape(-1)]).astype(BF16)
    all_tails = lax.all_gather(jnp.stack(tails), "fsdp")
    for l in range(LAYERS):
        tail = all_tails[:, l]
        gmod = tail[:, : n * 6 * d].reshape(owners * n, 6 * d)
        gbias = jnp.sum(tail[:, n * 6 * d :].astype(F32), axis=0)
        dada = dot_tn(lifted, gmod)
        lift_grad = lift_grad + dot_nt(gmod, ada_weight[l])
        small = []
        at = 0
        for size in (2 * d, d, ff, d):
            own = size // owners
            small.append(lax.dynamic_slice(gbias, (at + me * own,), (own,)))
            at += size
        dada_b = jnp.sum(gmod.astype(F32), axis=0)
        own = 6 * d // owners
        small.append(lax.dynamic_slice(dada_b, (me * own,), (own,)))
        small = jnp.concatenate(small)
        grads[l] = (dada.astype(BF16), small.astype(BF16))
    full_a = lax.all_gather(jnp.stack([t[0] for t in sums]), "rep", axis=2, tiled=True)
    full_f2 = lax.all_gather(jnp.stack([t[1] for t in sums]), "rep", axis=1, tiled=True)
    full_a = full_a.astype(F32)
    input_grad = g.reshape(latents.shape)

    gcond = lift_grad * (sig * (1.0 + cond * (1.0 - sig)))
    hi = gcond.astype(BF16)
    lo = (gcond - hi.astype(F32)).astype(BF16)
    both = jnp.concatenate([hi, lo], axis=1)
    w = cond.shape[1]

    def scatter_rows(hot):
        out = dot_tn(hot.astype(BF16), both)
        return (out[:, :w] + out[:, w:]).astype(BF16)

    tables = (scatter_rows(label_hot), scatter_rows(step_hot))
    grads, tables = lax.psum((grads, tables), "rep")

    def stack(f):
        return jnp.stack([f(grads[l]).astype(F32) for l in range(LAYERS)])

    sizes = [2 * d // owners, d // owners, ff // owners, d // owners, 6 * d // owners]
    offs = [sum(sizes[:i]) for i in range(6)]
    sm = [stack(lambda t, i=i: t[1][offs[i] : offs[i + 1]]) for i in range(5)]
    return (
        outputs,
        input_grad,
        tables[0].astype(F32),
        tables[1].astype(F32),
        stack(lambda t: t[0]),
        sm[4],
        full_a[:, :, : 3 * d],
        sm[0],
        full_a[:, :, 3 * d : 4 * d],
        sm[1],
        full_a[:, :, 4 * d :],
        sm[2],
        full_f2.astype(F32),
        sm[3],
    )


def solution(mesh):
    data = P(None, ("fsdp", "rep"), None, None)
    ids = P(None, ("fsdp", "rep"))
    two = P(None, "fsdp")
    three = P(None, "fsdp", None)
    layer = (three, two) * 5
    in_specs = (data, data, ids, ids, ids, two, two) + layer
    out_specs = (data, data, two, two) + layer
    return jax.shard_map(
        on_device, mesh=mesh, in_specs=in_specs, out_specs=out_specs, check_vma=False
    )
```

time: 2670 us -> 743 us (0.28)
  waiting for transfers between devices: 1370 us -> 415 us
  local copies, waits for them, and re-layouts: 386 us -> 15.7 us
  matrix products: 324 us -> 3.75 us
  other arithmetic: 267 us -> 14.1 us
  Pallas kernels: 0 us -> 153 us
  loops' own time: 84 us -> 0 us
  blocking collectives: 205 us -> 121 us
    reduce_scatter x7 -> x8, waiting for transfers between devices: 991 us -> 289 us  [the longest x2 121 us: on_device(): dwa = lax.psum_scatter(dwa, 'fsdp', scatter_dimension=0, tiled=True)]
    unnamed x22 -> x15, waiting for transfers between devices: 320 us -> 4.61 us
    dot_general x194 -> x10, matrix products: 274 us -> 3.75 us  [dot(): return lax.dot_general(a, b, (dims, ((), ())), preferred_element_type=F32)]
    all_gather x8 -> x3, blocking collectives: 200 us -> 45.1 us  [the longest x1 31.6 us: on_device(): all_tails = lax.all_gather(jnp.stack(tails), 'fsdp')]
    pallas_call x0 -> x4, Pallas kernels: none -> 153 us  [the longest x2 102 us: layer_backward(): pl.pallas_call(partial(bwd_kernel, first, last, d, ff), grid=(n,), in_spe...]
    cond x1220 -> x0, local copies, waits for them, and re-layouts: 123 us -> none
    add x76 -> x1, other arithmetic: 116 us -> 0.02 us  [on_device(): mod = mod.reshape(n, LAYERS, 6 * d) + ada_b[None]]
    another operation x18 -> x0, loops' own time: 84 us -> none  [the longest x3 73.4 us: on_device(): lax.scan(backward_step, totals, (saved, lifted, condition_vector, cotange...]
  transfers between devices with their start and end apart: 17 -> 15, of which waited for: 14 -> 11; matrix products, arithmetic and copies ran while one was open for 2% -> 8% of each run, Pallas kernels for 0% -> 10%
where the time goes in v1:
time: 743 us; the launch traced here: 742 us
  waiting for transfers between devices  415 us (56%)
  Pallas kernels  153 us (21%)
  blocking collectives  121 us (16%)
  between operations  15.8 us (2%)
  local copies, waits for them, and re-layouts  15.7 us (2%)
  other arithmetic  14.1 us (2%)
    reduce_scatter x2, waiting for transfers between devices, on_device(): dwa = lax.psum_scatter(dwa, 'fsdp', scatter_dimension=0, tiled=True)  121 us
    reduce_scatter x2, waiting for transfers between devices, on_device(): dwf2 = lax.psum_scatter(dwf2, 'fsdp', scatter_dimension=0, tiled=True)[0]  118 us
    pallas_call x2, Pallas kernels, layer_backward(): pl.pallas_call(partial(bwd_kernel, first, last, d, ff), grid=(n,), in_spe...  102 us
    unnamed x2, blocking collectives  70.1 us
    all_gather x2, waiting for transfers between devices, on_device(): wa.append(lax.all_gather(packed, 'fsdp', axis=0, tiled=True))  69.6 us
    pallas_call x2, Pallas kernels, layer_forward(): pl.pallas_call(partial(fwd_kernel, last, d, ff), grid=(n,), in_specs=[SME...  51.2 us
    reduce_scatter x2, waiting for transfers between devices, on_device(): dwa = lax.psum_scatter(dwa, 'rep', scatter_dimension=1, tiled=True)  48.9 us
    psum x1, waiting for transfers between devices, on_device(): grads, tables = lax.psum((grads, tables), 'rep')  34.5 us
  transfers between devices with their start and end apart: 15, of which 11 were waited for; matrix products, arithmetic and copies ran while one was open for 8% of the time, Pallas kernels for 10%

profile of v1, /device:TPU:0, one launch (start us, length us, event | category | flops | bytes accessed | tf_op | source)
XLA Modules:
  0.0 742.1 jit_solution(1773350428178278885)
XLA Ops:
  7.3 1.8 fusion.28
  9.1 0.8 slice_bitcast_fusion.4
  9.9 1.0 slice_bitcast_fusion
  11.1 0.7 pad_maximum_fusion.1
  11.9 0.7 all-gather.16.cloned.1.call-update
  12.6 0.7 pad_maximum_fusion.2
  15.9 39.5 %all-reduce = f32[10848]{0:T(1024)S(1)} all-reduce(f32[10848]{0:T(1024)S(1)} %dynamic-update-slice), channel_id=2, replica_groups=mesh['fsdp'=8,'rep'=4] {'fsdp'}, use_global_device_ids=true, to_apply=%add | all-reduce | flops 10848 | bytes 86784
  56.7 30.6 %fusion = f32[8,4608]{1,0:T(8,128)S(1)} fusion(f32[48,4608]{1,0:T(8,128)S(1)} %pad_maximum_fusion), kind=kCustom, calls=%all-reduce-scatter | all-reduce-scatter fusion | flops 294913 | bytes 1032704
  87.3 1.3 collective-permute-start
  88.7 2.5 collective-permute-start.1
  92.1 0.6 fusion.32
  92.9 0.6 reshape.231.live_ref
  94.3 2.6 collective-permute-done.1
  97.5 0.6 reshape_squeeze.6.mod_ref
  98.2 0.6 reshape_squeeze.7.mod_ref
  98.8 16.1 %all-gather.10.cloned.1.call-done.wa_ref = bf16[384,3072]{1,0:T(8,128)(2,1)} async-done(((bf16[48,3072]{1,0:T(8,128)(2,1)}), bf16[384,3072]{1,0:T(8,128)(2,1)}) %all-gather.10.cloned.1.call-update) | async-done | bytes 2359312 | tf_op jit(solution)/shard_map/all_gather | solution.py:260
  114.9 25.4 %layer_forward.2 = (f32[6,256,384]{2,1,0:T(8,128)}, bf16[6,256,1152]{2,1,0:T(8,128)(2,1)}, bf16[6,256,384]{2,1,0:T(8,128)(2,1)}, bf16[6,256,384]{2,1,0:T(8,128)(...) custom-call(s32[6]{0:T(128)} %reshape.231.live_ref, ...), custom_call_target="tpu_custom_call" | custom-call | tf_op jit(solution)/shard_map/layer_forward/pallas_call | solution.py:193
  140.3 17.5 %all-gather.16.cloned.1.call-done = bf16[1,1536,384]{2,1,0:T(8,128)(2,1)} async-done(((bf16[1,192,384]{2,1,0:T(8,128)(2,1)}), bf16[1,1536,384]{2,1,0:T(8,128)(2,1)}) %all-gather.16.cloned.1.call-update) | async-done | bytes 1179664 | tf_op jit(solution)/shard_map/all_gather | solution.py:261
  157.8 53.5 %all-gather.12.cloned.1.call-done.wa_ref = bf16[384,3072]{1,0:T(8,128)(2,1)} async-done(((bf16[48,3072]{1,0:T(8,128)(2,1)}), bf16[384,3072]{1,0:T(8,128)(2,1)}) %all-gather.12.cloned.1.call-update) | async-done | bytes 2359312 | tf_op jit(solution)/shard_map/all_gather | solution.py:260
  211.3 25.7 %layer_forward.3 = (bf16[6,256,384]{2,1,0:T(8,128)(2,1)}, bf16[6,256,1152]{2,1,0:T(8,128)(2,1)}, bf16[6,256,384]{2,1,0:T(8,128)(2,1)}, bf16[6,256,384]{2,1,0:T(8...) custom-call(s32[6]{0:T(128)} %reshape.231.live_ref, ...), custom_call_target="tpu_custom_call" | custom-call | tf_op jit(solution)/shard_map/layer_forward/pallas_call | solution.py:193
  237.0 50.9 %layer_backward.2 = (f32[6,256,384]{2,1,0:T(8,128)}, f32[6,6,384]{2,1,0:T(8,128)}, bf16[384,3072]{1,0:T(8,128)(2,1)}, bf16[1536,384]{1,0:T(8,128)(2,1)}, f32[1,3072]{1,0:T(1,128)}) custom-call(s32[6]{0:T(128)} %reshape.231.live_ref, bf16[6,256,384]{2,1,0:T(8,128)(2,1)} %bitcast.95, f32[6,256,384]{2,1,0:T(8,128)} %get-tuple-element.38.r_ref, ...), custom_call_target="tpu_custom_call" | custom-call | tf_op jit(solution)/shard_map/layer_backward/pallas_call | solution.py:220
  288.0 50.6 %layer_backward.3 = (bf16[6,256,384]{2,1,0:T(8,128)(2,1)}, f32[6,6,384]{2,1,0:T(8,128)}, bf16[384,3072]{1,0:T(8,128)(2,1)}, bf16[1536,384]{1,0:T(8,128)(2,1)}, f32[1,3072]{1,0:T(1,128)}) custom-call(s32[6]{0:T(128)} %reshape.231.live_ref, f32[6,256,384]{2,1,0:T(8,128)} %get-tuple-element.46.g_ref, bf16[6,256,384]{2,1,0:T(8,128)(2,1)} %bitcast.90, ...), custom_call_target="tpu_custom_call" | custom-call | tf_op jit(solution)/shard_map/layer_backward/pallas_call | solution.py:220
  339.9 31.6 %all-gather.4 = bf16[8,2,16896]{2,1,0:T(2,128)(2,1)S(1)} all-gather(bf16[1,2,16896]{2,1,0:T(2,128)(2,1)S(1)} %maximum_bitcast_fusion), channel_id=5, replica_groups=mesh['fsdp'=8,'rep'=4] {'fsdp'}, dimensions={0}, use_global_device_ids=true | all-gather | bytes 608256 | tf_op jit(solution)/shard_map/all_gather | solution.py:316
  371.5 0.8 fusion.27
  373.1 0.9 fusion.2
  374.0 0.9 fusion.1
  375.7 0.7 fusion.12
  376.6 0.7 fusion.11
  378.0 0.7 reduce-scatter.21.cloned.1.call-update
  378.8 20.0 %reduce-scatter.15.cloned.1.call-done = bf16[384,768]{1,0:T(8,128)(2,1)} async-done(((bf16[384,3072]{1,0:T(8,128)(2,1)}), bf16[384,768]{1,0:T(8,128)(2,1)}) %reduce-scatter.15.cloned.1.call-update) | async-done | bytes 589840 | tf_op jit(solution)/shard_map/reduce_scatter | solution.py:309
  399.8 5.7 all-reduce.3
  405.7 28.9 %reduce-scatter.11.cloned.1.call-done = bf16[384,768]{1,0:T(8,128)(2,1)} async-done(((bf16[384,3072]{1,0:T(8,128)(2,1)}), bf16[384,768]{1,0:T(8,128)(2,1)}) %reduce-scatter.11.cloned.1.call-update) | async-done | bytes 589840 | tf_op jit(solution)/shard_map/reduce_scatter | solution.py:309
  437.7 34.5 %all-reduce.7.cloned.1.call-done = (bf16[1000,48]{0,1:T(8,128)(2,1)}, bf16[1000,48]{0,1:T(8,128)(2,1)}, bf16[1,48,2304]{2,1,0:T(8,128)(2,1)}, bf16[1,48,2304]{2,1,0:T(8,128)(2,1)}) async-done(((bf16[1000,48]{0,1:T(8,128)(2,1)}, bf16[1000,48]{0,1:T(8,128)(2,1)}, bf16[1,48,2304]{2,1,0:T(8,128)(2,1)}, bf16[1,48,2304]{2,1,0:T(8,128)(2,1)}), (bf16[1000,48]{0,1:T(8,128)(2,1)}, bf16[1000,48]{0,1:T(8,128)(2,1)}, ...) | async-done | bytes 634384 | tf_op jit(solution)/shard_map/psum | solution.py:350
  472.3 1.6 convert_element_type.133
  473.8 1.6 convert_element_type.135
  475.4 2.0 maximum_convert_fusion
  477.4 57.1 %reduce-scatter.25.cloned.1.call-done = bf16[1,48,384]{2,1,0:T(8,128)(2,1)} async-done(((bf16[8,48,384]{2,1,0:T(8,128)(2,1)}), bf16[1,48,384]{2,1,0:T(8,128)(2,1)}) %reduce-scatter.25.cloned.1.call-update) | async-done | bytes 36880 | tf_op jit(solution)/shard_map/reduce_scatter | solution.py:313
  534.6 61.0 %reduce-scatter.21.cloned.1.call-done = bf16[1,48,384]{2,1,0:T(8,128)(2,1)} async-done(((bf16[8,48,384]{2,1,0:T(8,128)(2,1)}), bf16[1,48,384]{2,1,0:T(8,128)(2,1)}) %reduce-scatter.21.cloned.1.call-update) | async-done | bytes 36880 | tf_op jit(solution)/shard_map/reduce_scatter | solution.py:313
  595.6 0.8 pad_maximum_fusion.4
  596.4 5.9 all_gather.39
  602.3 0.9 convert_element_type.143
  603.1 56.7 %reduce-scatter.17.cloned.1.call-done = bf16[48,768]{1,0:T(8,128)(2,1)} async-done(((bf16[384,768]{1,0:T(8,128)(2,1)}), bf16[48,768]{1,0:T(8,128)(2,1)}) %reduce-scatter.17.cloned.1.call-update) | async-done | bytes 73744 | tf_op jit(solution)/shard_map/reduce_scatter | solution.py:310
  659.8 64.8 %reduce-scatter.13.cloned.1.call-done = bf16[48,768]{1,0:T(8,128)(2,1)} async-done(((bf16[384,768]{1,0:T(8,128)(2,1)}), bf16[48,768]{1,0:T(8,128)(2,1)}) %reduce-scatter.13.cloned.1.call-update) | async-done | bytes 73744 | tf_op jit(solution)/shard_map/reduce_scatter | solution.py:310
  724.6 0.9 pad_maximum_fusion.3
  725.6 7.6 %all_gather.38 = bf16[2,48,3072]{2,1,0:T(8,128)(2,1)S(1)} all-gather(bf16[2,48,768]{2,1,0:T(8,128)(2,1)S(1)} %pad_maximum_fusion.3), channel_id=1, replica_groups=mesh['fsdp'=8,'rep'=4] {'rep'}, dimensions={2}, use_global_device_ids=true | all-gather | bytes 737280 | tf_op jit(solution)/shard_map/all_gather | solution.py:334
  733.2 0.8 slice.199
  734.0 0.7 slice.200
  734.7 0.9 slice.201
  (165 shorter events, 13.1 us)
Async XLA Ops:
  7.2 48.8 %copy-start = (bf16[1000,48]{0,1:T(8,128)(2,1)S(1)}, bf16[1000,48]{0,1:T(8,128)(2,1)}, u32[]{:S(2)}) copy-start(bf16[1000,48]{0,1:T(8,128)(2,1)} %param.23) | copy-start | bytes 288004
  7.2 3.7 copy-start.3
  7.2 91.6 %all-gather.14.cloned.1.call-start = ((), (), s32[]{:S(2)}) async-start(), calls=%async_computation.18 | async-start | bytes 1327104 | tf_op jit(solution)/shard_map/all_gather | solution.py:261
  9.1 105.8 %all-gather.10.cloned.1.call-start = ((), (), s32[]{:S(2)}) async-start(), calls=%async_computation.8 | async-start | bytes 2654208 | tf_op jit(solution)/shard_map/all_gather | solution.py:260
  10.9 2.5 copy-start.11
  11.0 2.7 copy-start.12
  11.0 2.9 copy-start.9
  11.0 2.9 copy-start.15
  11.0 3.0 copy-start.16
  11.0 3.1 copy-start.10
  11.0 3.2 copy-start.17
  11.0 3.2 copy-start.8
  11.1 44.7 %copy-start.14 = (bf16[1000,48]{0,1:T(8,128)(2,1)S(1)}, bf16[1000,48]{0,1:T(8,128)(2,1)}, u32[]{:S(2)}) copy-start(bf16[1000,48]{0,1:T(8,128)(2,1)} %param.22) | copy-start | bytes 288004
  11.8 44.4 %copy-start.2 = (bf16[2,48,2304]{2,1,0:T(8,128)(2,1)S(1)}, bf16[2,48,2304]{2,1,0:T(8,128)(2,1)}, u32[]{:S(2)}) copy-start(bf16[2,48,2304]{2,1,0:T(8,128)(2,1)} %param.24) | copy-start | bytes 1327108
  11.8 146.0 %all-gather.16.cloned.1.call-start = ((), (), s32[]{:S(2)}) async-start(), calls=%async_computation.19 | async-start | bytes 1327104 | tf_op jit(solution)/shard_map/all_gather | solution.py:261
  12.6 198.7 %all-gather.12.cloned.1.call-start = ((), (), s32[]{:S(2)}) async-start(), calls=%async_computation.9 | async-start | bytes 2654208 | tf_op jit(solution)/shard_map/all_gather | solution.py:260
  13.4 364.0 %reduce-scatter.23.cloned.1.call-start = ((), (), s32[]{:S(2)}) async-start(), calls=%async_computation.16 | async-start | bytes 1474560 | tf_op jit(solution)/shard_map/reduce_scatter | solution.py:312
  56.7 36.0 %copy-start.13 = (s32[3,1]{0,1:T(1,128)S(1)}, s32[3,1]{0,1:T(1,128)}, u32[]{:S(2)}) copy-start(s32[3,1]{0,1:T(1,128)} %param.19) | copy-start | bytes 40
  87.3 9.6 %collective-permute-start = (f32[8,4608]{1,0:T(8,128)S(1)}, f32[8,4608]{1,0:T(8,128)S(1)}, u32[]{:S(2)}, u32[]{:S(2)}) collective-permute-start(f32[8,4608]{1,0:T(8,128)S(1)} %fusion), channel_id=1, source_target_pairs={{0,4},{4,8},{8,12},{12,16},{16,20},{20,24},{24,28},{1,5},{5,9},{9,... | collective-permute-start | bytes 442376
  88.7 8.3 %collective-permute-start.1 = (f32[6,4608]{1,0:T(8,128)S(1)}, f32[6,4608]{1,0:T(8,128)S(1)}, u32[]{:S(2)}, u32[]{:S(2)}) collective-permute-start(f32[6,4608]{1,0:T(8,128)S(1)} %slice.202), channel_id=1, source_target_pairs={{0,8},{4,12},{8,16},{12,20},{16,24},{20,28},{1,9},{5,13},{9,17},{1... | collective-permute-start | bytes 331784
  288.0 90.0 %reduce-scatter.19.cloned.1.call-start = ((), (), s32[]{:S(2)}) async-start(), calls=%async_computation.14 | async-start | bytes 1474560 | tf_op jit(solution)/shard_map/reduce_scatter | solution.py:312
  338.7 0.7 copy-start.6
  338.7 0.9 copy-start.4
  338.7 0.9 copy-start.7
  338.7 0.9 copy-start.5
  338.7 60.0 %reduce-scatter.15.cloned.1.call-start = ((), (), s32[]{:S(2)}) async-start(), calls=%async_computation.12 | async-start | bytes 2949120 | tf_op jit(solution)/shard_map/reduce_scatter | solution.py:309
  339.7 94.9 %reduce-scatter.11.cloned.1.call-start = ((), (), s32[]{:S(2)}) async-start(), calls=%async_computation.10 | async-start | bytes 2949120 | tf_op jit(solution)/shard_map/reduce_scatter | solution.py:309
  372.3 99.9 %all-reduce.7.cloned.1.call-start = ((), (), s32[]{:S(2)}) async-start(), calls=%async_computation.20 | async-start | bytes 1277952 | tf_op jit(solution)/shard_map/psum | solution.py:350
  377.3 157.2 %reduce-scatter.25.cloned.1.call-start = ((), (), s32[]{:S(2)}) async-start(), calls=%async_computation.17 | async-start | bytes 331776 | tf_op jit(solution)/shard_map/reduce_scatter | solution.py:313
  377.9 217.7 %reduce-scatter.21.cloned.1.call-start = ((), (), s32[]{:S(2)}) async-start(), calls=%async_computation.15 | async-start | bytes 331776 | tf_op jit(solution)/shard_map/reduce_scatter | solution.py:313
  378.7 281.2 %reduce-scatter.17.cloned.1.call-start = ((), (), s32[]{:S(2)}) async-start(), calls=%async_computation.13 | async-start | bytes 663552 | tf_op jit(solution)/shard_map/reduce_scatter | solution.py:310
  398.8 325.8 %reduce-scatter.13.cloned.1.call-start = ((), (), s32[]{:S(2)}) async-start(), calls=%async_computation.11 | async-start | bytes 663552 | tf_op jit(solution)/shard_map/reduce_scatter | solution.py:310
  725.6 10.0 %copy-start.1 = (bf16[1000,48]{0,1:T(8,128)(2,1)S(1)}, bf16[1000,48]{0,1:T(8,128)(2,1)}, u32[]{:S(2)}) copy-start(bf16[1000,48]{0,1:T(8,128)(2,1)} %param.23) | copy-start | bytes 288004
Sparse Core Ops, SparseCore 0:
  10.8 44.6 all-gather.13
  58.3 56.5 all-gather.9
  117.7 40.0 all-gather.15
  160.4 50.8 all-gather.11
  288.1 24.2 reduce-scatter.22
  338.8 24.2 reduce-scatter.18
  365.6 33.0 reduce-scatter.14
  401.5 33.0 reduce-scatter.10
  438.3 33.8 all-reduce.6
  475.4 59.1 reduce-scatter.24
  537.9 57.6 reduce-scatter.20
  598.7 61.0 reduce-scatter.16
  663.5 61.1 reduce-scatter.12
